TPU v7x, 512 devices: a whole 4x4x16 slice. The times are simulated.
512 devices in a mesh: gx: 32 (over x, z_hi, y), gy: 16 (over z_lo, core).
Axes of the slice: x: 4, y: 4, z: 16 (z_hi: 2, z_lo: 8; z = z_hi * 8 + z_lo), core: 2. Of those that a mesh axis runs over, the one named last changes fastest.
Arguments:
- start_vectors: bfloat16 [128, 32, 128, 128], P('gx', 'gy'), may hold values from -6 to 6
- blocks: bfloat16 [128, 32, 7, 128, 128], P('gx', 'gy'), as said below
- neighbour: int32 [128, 32, 7], P('gx', 'gy'), may hold values from 0 to 8, as said below
- counts: int32 [128, 32], P('gx', 'gy'), may hold values from 1 to 7, as said below
Outputs:
- moments: float32 [5, 128], replicated
- last_vector: bfloat16 [128, 32, 128, 128], P('gx', 'gy')
Inputs may be any that keep to these rules, and one draw needn't show every extreme that they name: `neighbour`: each tile's 7 slots name the codes 0, 1, 3, 4, 5, 7, 8 once each, its live slots first; code 4 (the tile itself) is always live; tile t couples to tile t + d through a live slot exactly when tile t + d couples to t through a live slot of the opposite code. `counts`: one plus the number of the tile's live couplings to other tiles. The block of a live coupling of tile t + d back to tile t is the transpose of the block of tile t towards t + d; blocks of code 4 are symmetric.
All inputs are finite; a program needn't handle non-finite values.
Results may differ from a plain program's by a relative error of at most 0.0045.
Values may be sent and summed in bfloat16 or wider, within the bound.
A program may use at most 64 MiB of HBM per device.

v0:
```python
import jax
import jax.numpy as jnp
from jax import lax
from jax.sharding import PartitionSpec as P

ITERS = 4


def with_halo(cells, sides, width):
    for axis, dim in sides:
        count = lax.axis_size(axis)
        head = lax.slice_in_dim(cells, 0, width, axis=dim)
        tail = lax.slice_in_dim(cells, cells.shape[dim] - width, cells.shape[dim], axis=dim)
        cells = jnp.concatenate(
            [
                lax.ppermute(tail, axis, [(i, (i + 1) % count) for i in range(count)]),
                cells,
                lax.ppermute(head, axis, [((i + 1) % count, i) for i in range(count)]),
            ],
            axis=dim,
        )
    return cells


def local_apply(extended, blocks, neighbour, counts):
    tiles_x, tiles_y, slots = neighbour.shape
    vectors, orbitals = (extended.shape[2], extended.shape[3])
    flat = extended.reshape((tiles_x + 2) * (tiles_y + 2), vectors, orbitals)
    xs = jnp.arange(tiles_x, dtype=jnp.int32)[:, None] + 1
    ys = jnp.arange(tiles_y, dtype=jnp.int32)[None, :] + 1
    total = jnp.zeros((tiles_x, tiles_y, vectors, orbitals), jnp.float32)
    for slot in range(slots):
        code = neighbour[:, :, slot]
        index = (xs + code // 3 - 1) * (tiles_y + 2) + (ys + code % 3 - 1)
        piece = jnp.take(flat, index, axis=0)
        product = jnp.einsum(
            "xyrb,xyba->xyra", piece, blocks[:, :, slot], preferred_element_type=jnp.float32
        )
        live = (slot < counts).astype(jnp.float32)[:, :, None, None]
        total = total + live * product
    return total


def extend(vectors):
    along_x = with_halo(vectors, (("gx", 0),), 1)
    return with_halo(along_x, (("gy", 1),), 1)


def on_device(start_vectors, blocks, neighbour, counts):
    tiles_x, tiles_y = counts.shape
    total_rows = (
        tiles_x * lax.axis_size("gx") * tiles_y * lax.axis_size("gy") * start_vectors.shape[3]
    )
    first = start_vectors.astype(jnp.float32)
    partials = [jnp.sum(first * first, axis=(0, 1, 3))]
    previous = first
    current = local_apply(extend(start_vectors), blocks, neighbour, counts)
    partials.append(jnp.sum(first * current, axis=(0, 1, 3)))
    for step in range(ITERS - 1):
        image = local_apply(extend(current.astype(jnp.bfloat16)), blocks, neighbour, counts)
        following = 2.0 * image - previous
        previous, current = (current, following)
        partials.append(jnp.sum(first * current, axis=(0, 1, 3)))
    summed = jnp.stack([lax.psum(term, ("gx", "gy")) for term in partials])
    return (summed / total_rows, current.astype(jnp.bfloat16))


def solution(mesh):
    in_specs = (
        P("gx", "gy", None, None),
        P("gx", "gy", None, None, None),
        P("gx", "gy", None),
        P("gx", "gy"),
    )
    out_specs = (P(), P("gx", "gy", None, None))
    return jax.shard_map(
        on_device, mesh=mesh, in_specs=in_specs, out_specs=out_specs, check_vma=False
    )
```

profile of v0, /device:TPU:1, one launch (start us, length us, event | category | flops | bytes accessed | tf_op | source)
XLA Modules:
  0.0 365.0 jit_solution(12642964493823538940)
XLA Ops:
  1.5 4.0 %collective-permute-start = (bf16[1,2,128,128]{3,2,1,0:T(8,128)(2,1)S(1)}, bf16[1,2,128,128]{3,2,1,0:T(8,128)(2,1)S(1)}, u32[]{:S(2)}, u32[]{:S(2)}) collective-permute-start(bf16[1,2,128,128]{3,2,1,0:T(8,128)(2,1)S(1)} %get-tuple-element.49), channel_id=1, source_target_pairs={{0,16},{16,32},{32,48},{48,64},{64,80},{80,96},{96,112},{112,128},... | collective-permute-start | bytes 196616 | tf_op jit(solution)/shard_map/ppermute | solution.py:16
  5.6 18.8 %collective-permute-start.1 = (bf16[1,2,128,128]{3,2,1,0:T(8,128)(2,1)S(1)}, bf16[1,2,128,128]{3,2,1,0:T(8,128)(2,1)S(1)}, u32[]{:S(2)}, u32[]{:S(2)}) collective-permute-start(bf16[1,2,128,128]{3,2,1,0:T(8,128)(2,1)S(1)} %get-tuple-element.48), channel_id=1, source_target_pairs={{16,0},{32,16},{48,32},{64,48},{80,64},{96,80},{112,96},{128,112},... | collective-permute-start | bytes 196616 | tf_op jit(solution)/shard_map/ppermute | solution.py:18
  32.2 4.7 %collective-permute-start.3 = (bf16[6,1,128,128]{3,2,1,0:T(8,128)(2,1)S(1)}, bf16[6,1,128,128]{3,2,1,0:T(8,128)(2,1)S(1)}, u32[]{:S(2)}, u32[]{:S(2)}) collective-permute-start(bf16[6,1,128,128]{3,2,1,0:T(8,128)(2,1)S(1)} %get-tuple-element.41), channel_id=1, source_target_pairs={{1,0},{2,1},{3,2},{4,3},{5,4},{6,5},{7,6},{8,7},{9,8},{10,9},{11,1... | collective-permute-start | bytes 589832 | tf_op jit(solution)/shard_map/ppermute | solution.py:18
  36.9 1.9 collective-permute-start.2
  39.2 5.3 %collective-permute-done.2 = bf16[6,1,128,128]{3,2,1,0:T(8,128)(2,1)S(1)} collective-permute-done((bf16[6,1,128,128]{3,2,1,0:T(8,128)(2,1)S(1)}, bf16[6,1,128,128]{3,2,1,0:T(8,128)(2,1)S(1)}, u32[]{:S(2)}, u32[]{:S(2)}) %collective-permute-start.2) | collective-permute-done | bytes 196640 | tf_op jit(solution)/shard_map/ppermute | solution.py:16
  45.9 1.3 gather_fusion.1
  51.6 1.4 convolution_multiply_fusion.27
  53.0 1.4 fusion.29
  56.4 12.2 %collective-permute-start.5 = (bf16[1,2,128,128]{2,3,1,0:T(8,128)(2,1)S(1)}, bf16[1,2,128,128]{2,3,1,0:T(8,128)(2,1)S(1)}, u32[]{:S(2)}, u32[]{:S(2)}) collective-permute-start(bf16[1,2,128,128]{2,3,1,0:T(8,128)(2,1)S(1)} %get-tuple-element.47), channel_id=1, source_target_pairs={{16,0},{32,16},{48,32},{64,48},{80,64},{96,80},{112,96},{128,112},... | collective-permute-start | bytes 196616 | tf_op jit(solution)/shard_map/ppermute | solution.py:18
  68.6 1.9 collective-permute-start.4
  70.5 2.8 collective-permute-done.5
  73.3 13.4 %collective-permute-done.4 = bf16[1,2,128,128]{2,3,1,0:T(8,128)(2,1)S(1)} collective-permute-done((bf16[1,2,128,128]{2,3,1,0:T(8,128)(2,1)S(1)}, bf16[1,2,128,128]{2,3,1,0:T(8,128)(2,1)S(1)}, u32[]{:S(2)}, u32[]{:S(2)}) %collective-permute-start.4) | collective-permute-done | bytes 65568 | tf_op jit(solution)/shard_map/ppermute | solution.py:16
  87.4 12.2 %collective-permute-start.7 = (bf16[6,1,128,128]{2,3,1,0:T(8,128)(2,1)}, bf16[6,1,128,128]{2,3,1,0:T(8,128)(2,1)S(1)}, u32[]{:S(2)}, u32[]{:S(2)}) collective-permute-start(bf16[6,1,128,128]{2,3,1,0:T(8,128)(2,1)} %get-tuple-element.39), channel_id=1, source_target_pairs={{1,0},{2,1},{3,2},{4,3},{5,4},{6,5},{7,6},{8,7},{9,8},{10,9},{11,1... | collective-permute-start | bytes 589832 | tf_op jit(solution)/shard_map/ppermute | solution.py:18
  99.6 1.9 collective-permute-start.6
  103.1 1.6 collective-permute-done.6
  106.6 1.4 gather_fusion.8
  108.0 1.4 gather_fusion.9
  109.4 1.4 gather_fusion.10
  110.8 1.4 gather_fusion.11
  112.2 1.4 gather_fusion.12
  115.8 1.4 convolution_multiply_fusion.20
  117.2 1.8 copy.264
  119.0 1.8 copy.265
  120.8 1.8 copy.266
  122.6 1.8 copy.267
  126.1 1.3 fusion.23
  127.5 1.4 fusion.22
  131.5 1.9 collective-permute-start.9
  133.5 3.4 collective-permute-start.8
  136.9 14.6 %collective-permute-done.8 = bf16[1,2,128,128]{2,3,1,0:T(8,128)(2,1)S(1)} collective-permute-done((bf16[1,2,128,128]{2,3,1,0:T(8,128)(2,1)S(1)}, bf16[1,2,128,128]{2,3,1,0:T(8,128)(2,1)S(1)}, u32[]{:S(2)}, u32[]{:S(2)}) %collective-permute-start.8) | collective-permute-done | bytes 65568 | tf_op jit(solution)/shard_map/ppermute | solution.py:16
  151.6 11.8 %collective-permute-start.11 = (bf16[6,1,128,128]{2,3,1,0:T(8,128)(2,1)S(1)}, bf16[6,1,128,128]{2,3,1,0:T(8,128)(2,1)S(1)}, u32[]{:S(2)}, u32[]{:S(2)}) collective-permute-start(bf16[6,1,128,128]{2,3,1,0:T(8,128)(2,1)S(1)} %get-tuple-element.37), channel_id=1, source_target_pairs={{1,0},{2,1},{3,2},{4,3},{5,4},{6,5},{7,6},{8,7},{9,8},{10,9},{11,1... | collective-permute-start | bytes 589832 | tf_op jit(solution)/shard_map/ppermute | solution.py:18
  163.3 1.9 collective-permute-start.10
  165.3 2.9 collective-permute-done.10
  170.9 1.3 gather_fusion.16
  172.2 1.3 gather_fusion.17
  173.5 1.3 gather_fusion.18
  176.0 1.3 gather_fusion.20
  177.3 1.8 copy.270
  179.2 1.3 convolution_multiply_fusion.13
  180.5 1.8 copy.271
  182.3 1.8 copy.272
  184.1 1.8 copy.273
  185.9 1.8 copy.274
  189.7 1.4 fusion.15
  191.1 1.4 fusion.14
  195.0 1.9 collective-permute-start.13
  196.9 3.4 collective-permute-start.12
  200.3 14.7 %collective-permute-done.12 = bf16[1,2,128,128]{2,3,1,0:T(8,128)(2,1)S(1)} collective-permute-done((bf16[1,2,128,128]{2,3,1,0:T(8,128)(2,1)S(1)}, bf16[1,2,128,128]{2,3,1,0:T(8,128)(2,1)S(1)}, u32[]{:S(2)}, u32[]{:S(2)}) %collective-permute-start.12) | collective-permute-done | bytes 65568 | tf_op jit(solution)/shard_map/ppermute | solution.py:16
  215.1 11.8 %collective-permute-start.15 = (bf16[6,1,128,128]{2,3,1,0:T(8,128)(2,1)S(1)}, bf16[6,1,128,128]{2,3,1,0:T(8,128)(2,1)S(1)}, u32[]{:S(2)}, u32[]{:S(2)}) collective-permute-start(bf16[6,1,128,128]{2,3,1,0:T(8,128)(2,1)S(1)} %get-tuple-element.35), channel_id=1, source_target_pairs={{1,0},{2,1},{3,2},{4,3},{5,4},{6,5},{7,6},{8,7},{9,8},{10,9},{11,1... | collective-permute-start | bytes 589832 | tf_op jit(solution)/shard_map/ppermute | solution.py:18
  226.9 2.1 collective-permute-start.14
  229.0 2.8 collective-permute-done.14
  233.2 1.3 gather_fusion.22
  237.0 1.3 gather_fusion.25
  238.3 1.3 gather_fusion.26
  239.6 1.3 gather_fusion.27
  240.9 1.8 copy.277
  242.7 1.3 convolution_multiply_fusion.6
  244.1 1.8 copy.278
  246.7 1.8 copy.280
  248.5 1.8 copy.281
  250.3 1.8 copy.282
  253.2 1.4 fusion.7
  254.6 1.4 fusion.6
  258.1 105.4 %all-reduce = (f32[1,128]{1,0:T(1,128)S(1)}, f32[1,128]{1,0:T(1,128)S(1)}, f32[1,128]{1,0:T(1,128)S(1)}, f32[1,128]{1,0:T(1,128)S(1)}, f32[1,128]{1,0:T(1,128)S(1)}) all-reduce(f32[1,128]{1,0:T(1,128)S(1)} %bitcast.259, f32[1,128]{1,0:T(1,128)S(1)} %bitcast.256, ...), channel_id=1, replica_groups=mesh['gx'=32,'gy'=16] {'gx','gy'}, use_global_device_ids=true, to_apply=%region_1.2 | all-reduce | flops 640 | bytes 5120 | tf_op jit(solution)/shard_map/psum | solution.py:64
  (245 shorter events, 45.2 us)
Async XLA Ops:
  1.5 29.6 %collective-permute-start = (bf16[1,2,128,128]{3,2,1,0:T(8,128)(2,1)S(1)}, bf16[1,2,128,128]{3,2,1,0:T(8,128)(2,1)S(1)}, u32[]{:S(2)}, u32[]{:S(2)}) collective-permute-start(bf16[1,2,128,128]{3,2,1,0:T(8,128)(2,1)S(1)} %get-tuple-element.49), channel_id=1, source_target_pairs={{0,16},{16,32},{32,48},{48,64},{64,80},{80,96},{96,112},{112,128},... | collective-permute-start | bytes 196616 | tf_op jit(solution)/shard_map/ppermute | solution.py:16
  5.6 26.5 %collective-permute-start.1 = (bf16[1,2,128,128]{3,2,1,0:T(8,128)(2,1)S(1)}, bf16[1,2,128,128]{3,2,1,0:T(8,128)(2,1)S(1)}, u32[]{:S(2)}, u32[]{:S(2)}) collective-permute-start(bf16[1,2,128,128]{3,2,1,0:T(8,128)(2,1)S(1)} %get-tuple-element.48), channel_id=1, source_target_pairs={{16,0},{32,16},{48,32},{64,48},{80,64},{96,80},{112,96},{128,112},... | collective-permute-start | bytes 196616 | tf_op jit(solution)/shard_map/ppermute | solution.py:18
  28.4 23.2 %copy-start.52 = (pred[4,2]{1,0:T(4,128)(4,1)}, pred[4,2]{1,0:T(4,128)(4,1)S(1)}, u32[]{:S(2)}) copy-start(pred[4,2]{1,0:T(4,128)(4,1)S(1)} %get-tuple-element.74) | copy-start | bytes 28
  28.4 27.2 %copy-start.50 = (pred[4,2]{1,0:T(4,128)(4,1)}, pred[4,2]{1,0:T(4,128)(4,1)S(1)}, u32[]{:S(2)}) copy-start(pred[4,2]{1,0:T(4,128)(4,1)S(1)} %get-tuple-element.21) | copy-start | bytes 28
  30.0 22.9 %copy-start.48 = (pred[4,2]{1,0:T(4,128)(4,1)}, pred[4,2]{1,0:T(4,128)(4,1)S(1)}, u32[]{:S(2)}) copy-start(pred[4,2]{1,0:T(4,128)(4,1)S(1)} %get-tuple-element.64) | copy-start | bytes 28
  30.0 24.3 %copy-start.46 = (pred[4,2]{1,0:T(4,128)(4,1)}, pred[4,2]{1,0:T(4,128)(4,1)S(1)}, u32[]{:S(2)}) copy-start(pred[4,2]{1,0:T(4,128)(4,1)S(1)} %get-tuple-element.66) | copy-start | bytes 28
  30.1 24.7 %copy-start.44 = (pred[4,2]{1,0:T(4,128)(4,1)}, pred[4,2]{1,0:T(4,128)(4,1)S(1)}, u32[]{:S(2)}) copy-start(pred[4,2]{1,0:T(4,128)(4,1)S(1)} %get-tuple-element.68) | copy-start | bytes 28
  30.1 25.1 %copy-start.42 = (pred[4,2]{1,0:T(4,128)(4,1)}, pred[4,2]{1,0:T(4,128)(4,1)S(1)}, u32[]{:S(2)}) copy-start(pred[4,2]{1,0:T(4,128)(4,1)S(1)} %get-tuple-element.70) | copy-start | bytes 28
  30.1 25.9 %copy-start.54 = (pred[4,2]{1,0:T(4,128)(4,1)}, pred[4,2]{1,0:T(4,128)(4,1)S(1)}, u32[]{:S(2)}) copy-start(pred[4,2]{1,0:T(4,128)(4,1)S(1)} %get-tuple-element.19) | copy-start | bytes 28
  30.9 25.0 %copy-start.26 = (f32[4,2]{1,0:T(4,128)}, f32[4,2]{1,0:T(4,128)S(1)}, u32[]{:S(2)}) copy-start(f32[4,2]{1,0:T(4,128)S(1)} %copy.253) | copy-start | bytes 100
  31.0 14.9 %copy-start.30 = (s32[1024]{0:T(1024)}, s32[1024]{0:T(1024)S(1)}, u32[]{:S(2)}) copy-start(s32[1024]{0:T(1024)S(1)} %get-tuple-element.100) | copy-start | bytes 12292
  31.0 16.2 %copy-start.28 = (s32[1024]{0:T(1024)}, s32[1024]{0:T(1024)S(1)}, u32[]{:S(2)}) copy-start(s32[1024]{0:T(1024)S(1)} %get-tuple-element.99) | copy-start | bytes 12292
  31.0 17.5 %copy-start.34 = (s32[1024]{0:T(1024)}, s32[1024]{0:T(1024)S(1)}, u32[]{:S(2)}) copy-start(s32[1024]{0:T(1024)S(1)} %get-tuple-element.98) | copy-start | bytes 12292
  31.0 18.7 %copy-start.32 = (s32[1024]{0:T(1024)}, s32[1024]{0:T(1024)S(1)}, u32[]{:S(2)}) copy-start(s32[1024]{0:T(1024)S(1)} %get-tuple-element.97) | copy-start | bytes 12292
  31.0 19.3 %copy-start.38 = (s32[1024]{0:T(1024)}, s32[1024]{0:T(1024)S(1)}, u32[]{:S(2)}) copy-start(s32[1024]{0:T(1024)S(1)} %get-tuple-element.96) | copy-start | bytes 12292
  31.0 19.9 %copy-start.36 = (s32[1024]{0:T(1024)}, s32[1024]{0:T(1024)S(1)}, u32[]{:S(2)}) copy-start(s32[1024]{0:T(1024)S(1)} %get-tuple-element.95) | copy-start | bytes 12292
  31.1 14.8 %copy-start.40 = (s32[1024]{0:T(1024)}, s32[1024]{0:T(1024)S(1)}, u32[]{:S(2)}) copy-start(s32[1024]{0:T(1024)S(1)} %pad_clamp_fusion.6) | copy-start | bytes 12292
  32.2 7.1 %collective-permute-start.3 = (bf16[6,1,128,128]{3,2,1,0:T(8,128)(2,1)S(1)}, bf16[6,1,128,128]{3,2,1,0:T(8,128)(2,1)S(1)}, u32[]{:S(2)}, u32[]{:S(2)}) collective-permute-start(bf16[6,1,128,128]{3,2,1,0:T(8,128)(2,1)S(1)} %get-tuple-element.41), channel_id=1, source_target_pairs={{1,0},{2,1},{3,2},{4,3},{5,4},{6,5},{7,6},{8,7},{9,8},{10,9},{11,1... | collective-permute-start | bytes 589832 | tf_op jit(solution)/shard_map/ppermute | solution.py:18
  36.9 7.6 %collective-permute-start.2 = (bf16[6,1,128,128]{3,2,1,0:T(8,128)(2,1)S(1)}, bf16[6,1,128,128]{3,2,1,0:T(8,128)(2,1)S(1)}, u32[]{:S(2)}, u32[]{:S(2)}) collective-permute-start(bf16[6,1,128,128]{3,2,1,0:T(8,128)(2,1)S(1)} %get-tuple-element.40), channel_id=1, source_target_pairs={{0,1},{1,2},{2,3},{3,4},{4,5},{5,6},{6,7},{7,8},{8,9},{9,10},{10,1... | collective-permute-start | bytes 589832 | tf_op jit(solution)/shard_map/ppermute | solution.py:16
  38.8 12.7 %copy-start.24 = (f32[4,2]{1,0:T(4,128)}, f32[4,2]{1,0:T(4,128)S(1)}, u32[]{:S(2)}) copy-start(f32[4,2]{1,0:T(4,128)S(1)} %get-tuple-element.59) | copy-start | bytes 100
  38.8 15.9 %copy-start.22 = (f32[4,2]{1,0:T(4,128)}, f32[4,2]{1,0:T(4,128)S(1)}, u32[]{:S(2)}) copy-start(f32[4,2]{1,0:T(4,128)S(1)} %get-tuple-element.58) | copy-start | bytes 100
  44.6 7.0 %copy-start = (bf16[4,2,7,128,128]{4,3,2,1,0:T(8,128)(2,1)S(1)}, bf16[4,2,7,128,128]{4,3,2,1,0:T(8,128)(2,1)}, u32[]{:S(2)}) copy-start(bf16[4,2,7,128,128]{4,3,2,1,0:T(8,128)(2,1)} %param.7) | copy-start | bytes 5505028
  51.6 2.8 copy-start.19
  53.0 1.8 copy-start.14
  55.9 45.6 %copy-start.4 = (bf16[4,2,128,128]{3,2,1,0:T(8,128)(2,1)S(1)}, bf16[4,2,128,128]{3,2,1,0:T(8,128)(2,1)}, u32[]{:S(2)}) copy-start(bf16[4,2,128,128]{3,2,1,0:T(8,128)(2,1)} %param.6) | copy-start | bytes 786436
  56.4 16.9 %collective-permute-start.5 = (bf16[1,2,128,128]{2,3,1,0:T(8,128)(2,1)S(1)}, bf16[1,2,128,128]{2,3,1,0:T(8,128)(2,1)S(1)}, u32[]{:S(2)}, u32[]{:S(2)}) collective-permute-start(bf16[1,2,128,128]{2,3,1,0:T(8,128)(2,1)S(1)} %get-tuple-element.47), channel_id=1, source_target_pairs={{16,0},{32,16},{48,32},{64,48},{80,64},{96,80},{112,96},{128,112},... | collective-permute-start | bytes 196616 | tf_op jit(solution)/shard_map/ppermute | solution.py:18
  68.6 18.1 %collective-permute-start.4 = (bf16[1,2,128,128]{2,3,1,0:T(8,128)(2,1)S(1)}, bf16[1,2,128,128]{2,3,1,0:T(8,128)(2,1)S(1)}, u32[]{:S(2)}, u32[]{:S(2)}) collective-permute-start(bf16[1,2,128,128]{2,3,1,0:T(8,128)(2,1)S(1)} %get-tuple-element.46), channel_id=1, source_target_pairs={{0,16},{16,32},{32,48},{48,64},{64,80},{80,96},{96,112},{112,128},... | collective-permute-start | bytes 196616 | tf_op jit(solution)/shard_map/ppermute | solution.py:16
  87.4 15.0 %collective-permute-start.7 = (bf16[6,1,128,128]{2,3,1,0:T(8,128)(2,1)}, bf16[6,1,128,128]{2,3,1,0:T(8,128)(2,1)S(1)}, u32[]{:S(2)}, u32[]{:S(2)}) collective-permute-start(bf16[6,1,128,128]{2,3,1,0:T(8,128)(2,1)} %get-tuple-element.39), channel_id=1, source_target_pairs={{1,0},{2,1},{3,2},{4,3},{5,4},{6,5},{7,6},{8,7},{9,8},{10,9},{11,1... | collective-permute-start | bytes 589832 | tf_op jit(solution)/shard_map/ppermute | solution.py:18
  99.6 5.1 %collective-permute-start.6 = (bf16[6,1,128,128]{2,3,1,0:T(8,128)(2,1)S(1)}, bf16[6,1,128,128]{2,3,1,0:T(8,128)(2,1)}, u32[]{:S(2)}, u32[]{:S(2)}) collective-permute-start(bf16[6,1,128,128]{2,3,1,0:T(8,128)(2,1)S(1)} %get-tuple-element.38), channel_id=1, source_target_pairs={{0,1},{1,2},{2,3},{3,4},{4,5},{5,6},{6,7},{7,8},{8,9},{9,10},{10,1... | collective-permute-start | bytes 589832 | tf_op jit(solution)/shard_map/ppermute | solution.py:16
  105.8 7.8 %copy-start.37 = (s32[1024]{0:T(1024)S(1)}, s32[1024]{0:T(1024)}, u32[]{:S(2)}) copy-start(s32[1024]{0:T(1024)} %copy-done.36) | copy-start | bytes 12292
  106.6 9.2 %copy-start.25 = (f32[4,2]{1,0:T(4,128)S(1)}, f32[4,2]{1,0:T(4,128)}, u32[]{:S(2)}) copy-start(f32[4,2]{1,0:T(4,128)} %copy-done.24) | copy-start | bytes 100
  106.6 9.2 %copy-start.53 = (pred[4,2]{1,0:T(4,128)(4,1)S(1)}, pred[4,2]{1,0:T(4,128)(4,1)}, u32[]{:S(2)}) copy-start(pred[4,2]{1,0:T(4,128)(4,1)} %copy-done.52) | copy-start | bytes 28
  114.9 9.5 %copy-start.7 = (bf16[8,128,128]{1,2,0:T(8,128)(2,1)S(1)}, bf16[8,128,128]{1,2,0:T(8,128)(2,1)}, u32[]{:S(2)}) copy-start(bf16[8,128,128]{1,2,0:T(8,128)(2,1)} %gather_fusion.12) | copy-start | bytes 786436
  115.8 9.5 %copy-start.6 = (bf16[8,128,128]{1,2,0:T(8,128)(2,1)S(1)}, bf16[8,128,128]{1,2,0:T(8,128)(2,1)}, u32[]{:S(2)}) copy-start(bf16[8,128,128]{1,2,0:T(8,128)(2,1)} %gather_fusion.13) | copy-start | bytes 786436
  117.2 8.9 %copy-start.49 = (pred[4,2]{1,0:T(4,128)(4,1)S(1)}, pred[4,2]{1,0:T(4,128)(4,1)}, u32[]{:S(2)}) copy-start(pred[4,2]{1,0:T(4,128)(4,1)} %copy-done.48) | copy-start | bytes 28
  120.8 6.7 %copy-start.47 = (pred[4,2]{1,0:T(4,128)(4,1)S(1)}, pred[4,2]{1,0:T(4,128)(4,1)}, u32[]{:S(2)}) copy-start(pred[4,2]{1,0:T(4,128)(4,1)} %copy-done.46) | copy-start | bytes 28
  125.2 3.6 copy-start.17
  125.2 3.6 copy-start.23
  125.2 3.6 copy-start.45
  127.4 1.9 copy-start.15
  127.4 1.9 copy-start.43
  129.3 1.0 copy-start.20
  131.5 36.8 %copy-start.41 = (s32[1024]{0:T(1024)S(1)}, s32[1024]{0:T(1024)}, u32[]{:S(2)}) copy-start(s32[1024]{0:T(1024)} %copy-done.40) | copy-start | bytes 12292
  131.5 5.3 %collective-permute-start.9 = (bf16[1,2,128,128]{2,3,1,0:T(8,128)(2,1)S(1)}, bf16[1,2,128,128]{2,3,1,0:T(8,128)(2,1)S(1)}, u32[]{:S(2)}, u32[]{:S(2)}) collective-permute-start(bf16[1,2,128,128]{2,3,1,0:T(8,128)(2,1)S(1)} %get-tuple-element.45), channel_id=1, source_target_pairs={{16,0},{32,16},{48,32},{64,48},{80,64},{96,80},{112,96},{128,112},... | collective-permute-start | bytes 196616 | tf_op jit(solution)/shard_map/ppermute | solution.py:18
  133.5 36.1 %copy-start.31 = (s32[1024]{0:T(1024)S(1)}, s32[1024]{0:T(1024)}, u32[]{:S(2)}) copy-start(s32[1024]{0:T(1024)} %copy-done.30) | copy-start | bytes 12292
  133.5 18.0 %collective-permute-start.8 = (bf16[1,2,128,128]{2,3,1,0:T(8,128)(2,1)S(1)}, bf16[1,2,128,128]{2,3,1,0:T(8,128)(2,1)S(1)}, u32[]{:S(2)}, u32[]{:S(2)}) collective-permute-start(bf16[1,2,128,128]{2,3,1,0:T(8,128)(2,1)S(1)} %get-tuple-element.44), channel_id=1, source_target_pairs={{0,16},{16,32},{32,48},{48,64},{64,80},{80,96},{96,112},{112,128},... | collective-permute-start | bytes 196616 | tf_op jit(solution)/shard_map/ppermute | solution.py:16
  151.5 19.4 %copy-start.29 = (s32[1024]{0:T(1024)S(1)}, s32[1024]{0:T(1024)}, u32[]{:S(2)}) copy-start(s32[1024]{0:T(1024)} %copy-done.28) | copy-start | bytes 12292
  151.5 20.7 %copy-start.35 = (s32[1024]{0:T(1024)S(1)}, s32[1024]{0:T(1024)}, u32[]{:S(2)}) copy-start(s32[1024]{0:T(1024)} %copy-done.34) | copy-start | bytes 12292
  151.6 13.7 %collective-permute-start.11 = (bf16[6,1,128,128]{2,3,1,0:T(8,128)(2,1)S(1)}, bf16[6,1,128,128]{2,3,1,0:T(8,128)(2,1)S(1)}, u32[]{:S(2)}, u32[]{:S(2)}) collective-permute-start(bf16[6,1,128,128]{2,3,1,0:T(8,128)(2,1)S(1)} %get-tuple-element.37), channel_id=1, source_target_pairs={{1,0},{2,1},{3,2},{4,3},{5,4},{6,5},{7,6},{8,7},{9,8},{10,9},{11,1... | collective-permute-start | bytes 589832 | tf_op jit(solution)/shard_map/ppermute | solution.py:18
  163.3 10.2 %copy-start.33 = (s32[1024]{0:T(1024)S(1)}, s32[1024]{0:T(1024)}, u32[]{:S(2)}) copy-start(s32[1024]{0:T(1024)} %copy-done.32) | copy-start | bytes 12292
  163.3 11.4 %copy-start.39 = (s32[1024]{0:T(1024)S(1)}, s32[1024]{0:T(1024)}, u32[]{:S(2)}) copy-start(s32[1024]{0:T(1024)} %copy-done.38) | copy-start | bytes 12292
  163.3 4.9 %collective-permute-start.10 = (bf16[6,1,128,128]{2,3,1,0:T(8,128)(2,1)S(1)}, bf16[6,1,128,128]{2,3,1,0:T(8,128)(2,1)S(1)}, u32[]{:S(2)}, u32[]{:S(2)}) collective-permute-start(bf16[6,1,128,128]{2,3,1,0:T(8,128)(2,1)S(1)} %get-tuple-element.36), channel_id=1, source_target_pairs={{0,1},{1,2},{2,3},{3,4},{4,5},{5,6},{6,7},{7,8},{8,9},{9,10},{10,1... | collective-permute-start | bytes 589832 | tf_op jit(solution)/shard_map/ppermute | solution.py:16
  177.3 10.4 %copy-start.8 = (bf16[8,128,128]{1,2,0:T(8,128)(2,1)S(1)}, bf16[8,128,128]{1,2,0:T(8,128)(2,1)}, u32[]{:S(2)}) copy-start(bf16[8,128,128]{1,2,0:T(8,128)(2,1)} %gather_fusion.19) | copy-start | bytes 786436
  189.7 2.8 copy-start.18
  191.1 1.8 copy-start.16
  195.0 5.3 %collective-permute-start.13 = (bf16[1,2,128,128]{2,3,1,0:T(8,128)(2,1)S(1)}, bf16[1,2,128,128]{2,3,1,0:T(8,128)(2,1)S(1)}, u32[]{:S(2)}, u32[]{:S(2)}) collective-permute-start(bf16[1,2,128,128]{2,3,1,0:T(8,128)(2,1)S(1)} %get-tuple-element.43), channel_id=1, source_target_pairs={{16,0},{32,16},{48,32},{64,48},{80,64},{96,80},{112,96},{128,112},... | collective-permute-start | bytes 196616 | tf_op jit(solution)/shard_map/ppermute | solution.py:18
  196.9 18.1 %collective-permute-start.12 = (bf16[1,2,128,128]{2,3,1,0:T(8,128)(2,1)S(1)}, bf16[1,2,128,128]{2,3,1,0:T(8,128)(2,1)S(1)}, u32[]{:S(2)}, u32[]{:S(2)}) collective-permute-start(bf16[1,2,128,128]{2,3,1,0:T(8,128)(2,1)S(1)} %get-tuple-element.42), channel_id=1, source_target_pairs={{0,16},{16,32},{32,48},{48,64},{64,80},{80,96},{96,112},{112,128},... | collective-permute-start | bytes 196616 | tf_op jit(solution)/shard_map/ppermute | solution.py:16
  215.1 13.9 %collective-permute-start.15 = (bf16[6,1,128,128]{2,3,1,0:T(8,128)(2,1)S(1)}, bf16[6,1,128,128]{2,3,1,0:T(8,128)(2,1)S(1)}, u32[]{:S(2)}, u32[]{:S(2)}) collective-permute-start(bf16[6,1,128,128]{2,3,1,0:T(8,128)(2,1)S(1)} %get-tuple-element.35), channel_id=1, source_target_pairs={{1,0},{2,1},{3,2},{4,3},{5,4},{6,5},{7,6},{8,7},{9,8},{10,9},{11,1... | collective-permute-start | bytes 589832 | tf_op jit(solution)/shard_map/ppermute | solution.py:18
  226.9 4.9 %collective-permute-start.14 = (bf16[6,1,128,128]{2,3,1,0:T(8,128)(2,1)S(1)}, bf16[6,1,128,128]{2,3,1,0:T(8,128)(2,1)S(1)}, u32[]{:S(2)}, u32[]{:S(2)}) collective-permute-start(bf16[6,1,128,128]{2,3,1,0:T(8,128)(2,1)S(1)} %get-tuple-element.34), channel_id=1, source_target_pairs={{0,1},{1,2},{2,3},{3,4},{4,5},{5,6},{6,7},{7,8},{8,9},{9,10},{10,1... | collective-permute-start | bytes 589832 | tf_op jit(solution)/shard_map/ppermute | solution.py:16
  240.9 5.0 %copy-start.5 = (bf16[8,128,128]{1,2,0:T(8,128)(2,1)S(1)}, bf16[8,128,128]{1,2,0:T(8,128)(2,1)}, u32[]{:S(2)}) copy-start(bf16[8,128,128]{1,2,0:T(8,128)(2,1)} %gather_fusion.23) | copy-start | bytes 786436
  253.2 2.8 copy-start.11
  254.6 1.8 copy-start.10
  256.4 1.1 copy-start.2
  256.4 1.2 copy-start.3
  (8 other events, 7.5 us)
where the time goes:
time: 367 us; the launch traced here: 365 us
  blocking collectives  105 us (29%)
  starting transfers between devices  95.8 us (26%)
  local copies, waits for them, and re-layouts  77.4 us (21%)
  waiting for transfers between devices  58.4 us (16%)
  matrix products  23.2 us (6%)
    psum x1, blocking collectives, on_device(): summed = jnp.stack([lax.psum(term, ('gx', 'gy')) for term in partials])  105 us
    ppermute x8, starting transfers between devices, with_halo(): lax.ppermute(head, axis, [((i + 1) % count, i) for i in range(count)])  75.3 us
    gather x49, local copies, waits for them, and re-layouts, local_apply(): piece = jnp.take(flat, index, axis=0)  65.7 us
    ppermute x8, waiting for transfers between devices, with_halo(): lax.ppermute(tail, axis, [(i, (i + 1) % count) for i in range(count)])  55.2 us
    dot_general x28, matrix products, local_apply(): jnp.einsum('xyrb,xyba->xyra', piece, blocks[:, :, slot], preferred_elemen...  23.2 us
    ppermute x8, starting transfers between devices, with_halo(): lax.ppermute(tail, axis, [(i, (i + 1) % count) for i in range(count)])  20.5 us
  transfers between devices with their start and end apart: 16, of which 9 were waited for; matrix products, arithmetic and copies ran while one was open for 2% of the time, Pallas kernels for 0%

commit v1 on v0

--- a/solution.py
+++ b/solution.py
@@ -61,7 +61,7 @@
         following = 2.0 * image - previous
         previous, current = (current, following)
         partials.append(jnp.sum(first * current, axis=(0, 1, 3)))
-    summed = jnp.stack([lax.psum(term, ("gx", "gy")) for term in partials])
+    summed = jnp.stack([lax.psum(lax.psum(term, "gy"), "gx") for term in partials])
     return (summed / total_rows, current.astype(jnp.bfloat16))
 
 

time: 367 us -> 461 us (1.26)
  the two profiles are of different devices: /device:TPU:1 before, /device:TPU:8 now
where the time goes in v1:
time: 461 us; the launch traced here: 459 us
  blocking collectives  205 us (44%)
  starting transfers between devices  86 us (19%)
  local copies, waits for them, and re-layouts  77.6 us (17%)
  waiting for transfers between devices  63 us (14%)
  matrix products  23.2 us (5%)
    psum x1, blocking collectives, on_device(): lax.psum(lax.psum(term, 'gy'), 'gx')  160 us
    ppermute x8, starting transfers between devices, with_halo(): lax.ppermute(head, axis, [((i + 1) % count, i) for i in range(count)])  67.5 us
    gather x49, local copies, waits for them, and re-layouts, local_apply(): piece = jnp.take(flat, index, axis=0)  66 us
    ppermute x8, waiting for transfers between devices, with_halo(): lax.ppermute(tail, axis, [(i, (i + 1) % count) for i in range(count)])  59.3 us
    psum x1, blocking collectives, on_device(): lax.psum(term, 'gy')  45.1 us
    dot_general x28, matrix products, local_apply(): jnp.einsum('xyrb,xyba->xyra', piece, blocks[:, :, slot], preferred_elemen...  23.2 us
    ppermute x8, starting transfers between devices, with_halo(): lax.ppermute(tail, axis, [(i, (i + 1) % count) for i in range(count)])  18.6 us
  transfers between devices with their start and end apart: 16, of which 11 were waited for; matrix products, arithmetic and copies ran while one was open for 2% of the time, Pallas kernels for 0%

profile of v1, /device:TPU:8, one launch (start us, length us, event | category | flops | bytes accessed | tf_op | source)
XLA Modules:
  0.0 459.4 jit_solution(13410557057187684822)
XLA Ops:
  1.5 3.5 collective-permute-start
  5.0 6.2 %collective-permute-start.1 = (bf16[1,2,128,128]{3,2,1,0:T(8,128)(2,1)S(1)}, bf16[1,2,128,128]{3,2,1,0:T(8,128)(2,1)S(1)}, u32[]{:S(2)}, u32[]{:S(2)}) collective-permute-start(bf16[1,2,128,128]{3,2,1,0:T(8,128)(2,1)S(1)} %get-tuple-element.53), channel_id=1, source_target_pairs={{16,0},{32,16},{48,32},{64,48},{80,64},{96,80},{112,96},{128,112},... | collective-permute-start | bytes 196616 | tf_op jit(solution)/shard_map/ppermute | solution.py:18
  19.0 8.2 %collective-permute-start.3 = (bf16[6,1,128,128]{3,2,1,0:T(8,128)(2,1)S(1)}, bf16[6,1,128,128]{3,2,1,0:T(8,128)(2,1)S(1)}, u32[]{:S(2)}, u32[]{:S(2)}) collective-permute-start(bf16[6,1,128,128]{3,2,1,0:T(8,128)(2,1)S(1)} %get-tuple-element.46), channel_id=1, source_target_pairs={{1,0},{2,1},{3,2},{4,3},{5,4},{6,5},{7,6},{8,7},{9,8},{10,9},{11,1... | collective-permute-start | bytes 589832 | tf_op jit(solution)/shard_map/ppermute | solution.py:18
  27.2 1.9 collective-permute-start.2
  30.4 10.4 %collective-permute-done.2 = bf16[6,1,128,128]{3,2,1,0:T(8,128)(2,1)S(1)} collective-permute-done((bf16[6,1,128,128]{3,2,1,0:T(8,128)(2,1)S(1)}, bf16[6,1,128,128]{3,2,1,0:T(8,128)(2,1)S(1)}, u32[]{:S(2)}, u32[]{:S(2)}) %collective-permute-start.2) | collective-permute-done | bytes 196640 | tf_op jit(solution)/shard_map/ppermute | solution.py:16
  42.2 1.3 gather_fusion.1
  48.0 1.4 convolution_multiply_fusion.27
  49.3 1.4 fusion.29
  52.7 15.3 %collective-permute-start.5 = (bf16[1,2,128,128]{2,3,1,0:T(8,128)(2,1)S(1)}, bf16[1,2,128,128]{2,3,1,0:T(8,128)(2,1)S(1)}, u32[]{:S(2)}, u32[]{:S(2)}) collective-permute-start(bf16[1,2,128,128]{2,3,1,0:T(8,128)(2,1)S(1)} %get-tuple-element.52), channel_id=1, source_target_pairs={{16,0},{32,16},{48,32},{64,48},{80,64},{96,80},{112,96},{128,112},... | collective-permute-start | bytes 196616 | tf_op jit(solution)/shard_map/ppermute | solution.py:18
  68.0 1.9 collective-permute-start.4
  70.0 10.8 %collective-permute-done.4 = bf16[1,2,128,128]{2,3,1,0:T(8,128)(2,1)S(1)} collective-permute-done((bf16[1,2,128,128]{2,3,1,0:T(8,128)(2,1)S(1)}, bf16[1,2,128,128]{2,3,1,0:T(8,128)(2,1)S(1)}, u32[]{:S(2)}, u32[]{:S(2)}) %collective-permute-start.4) | collective-permute-done | bytes 65568 | tf_op jit(solution)/shard_map/ppermute | solution.py:16
  81.5 1.9 collective-permute-start.7
  83.4 2.4 collective-permute-start.6
  88.0 9.0 %collective-permute-done.6 = bf16[6,1,128,128]{2,3,1,0:T(8,128)(2,1)} collective-permute-done((bf16[6,1,128,128]{2,3,1,0:T(8,128)(2,1)S(1)}, bf16[6,1,128,128]{2,3,1,0:T(8,128)(2,1)}, u32[]{:S(2)}, u32[]{:S(2)}) %collective-permute-start.6) | collective-permute-done | bytes 196640 | tf_op jit(solution)/shard_map/ppermute | solution.py:16
  99.0 1.4 gather_fusion.8
  100.4 1.4 gather_fusion.9
  101.8 1.4 gather_fusion.10
  103.3 1.4 gather_fusion.11
  104.7 1.4 gather_fusion.12
  108.3 1.4 convolution_multiply_fusion.20
  109.6 1.8 copy.264
  111.4 1.8 copy.265
  113.3 1.8 copy.266
  115.1 1.8 copy.267
  118.6 1.3 fusion.23
  120.0 1.4 fusion.22
  124.1 17.1 %collective-permute-start.9 = (bf16[1,2,128,128]{2,3,1,0:T(8,128)(2,1)S(1)}, bf16[1,2,128,128]{2,3,1,0:T(8,128)(2,1)S(1)}, u32[]{:S(2)}, u32[]{:S(2)}) collective-permute-start(bf16[1,2,128,128]{2,3,1,0:T(8,128)(2,1)S(1)} %get-tuple-element.50), channel_id=1, source_target_pairs={{16,0},{32,16},{48,32},{64,48},{80,64},{96,80},{112,96},{128,112},... | collective-permute-start | bytes 196616 | tf_op jit(solution)/shard_map/ppermute | solution.py:18
  141.2 1.9 collective-permute-start.8
  143.1 4.2 collective-permute-done.8
  147.5 1.9 collective-permute-start.11
  149.4 2.4 collective-permute-start.10
  152.8 10.2 %collective-permute-done.10 = bf16[6,1,128,128]{2,3,1,0:T(8,128)(2,1)S(1)} collective-permute-done((bf16[6,1,128,128]{2,3,1,0:T(8,128)(2,1)S(1)}, bf16[6,1,128,128]{2,3,1,0:T(8,128)(2,1)S(1)}, u32[]{:S(2)}, u32[]{:S(2)}) %collective-permute-start.10) | collective-permute-done | bytes 196640 | tf_op jit(solution)/shard_map/ppermute | solution.py:16
  165.7 1.3 gather_fusion.16
  167.0 1.3 gather_fusion.17
  168.3 1.3 gather_fusion.18
  169.6 1.3 gather_fusion.19
  170.9 1.3 gather_fusion.20
  172.2 1.8 copy.270
  174.0 1.3 convolution_multiply_fusion.13
  175.4 1.8 copy.271
  177.2 1.8 copy.272
  179.0 1.8 copy.273
  180.8 1.8 copy.274
  184.6 1.4 fusion.15
  186.0 1.4 fusion.14
  189.9 15.0 %collective-permute-start.13 = (bf16[1,2,128,128]{2,3,1,0:T(8,128)(2,1)S(1)}, bf16[1,2,128,128]{2,3,1,0:T(8,128)(2,1)S(1)}, u32[]{:S(2)}, u32[]{:S(2)}) collective-permute-start(bf16[1,2,128,128]{2,3,1,0:T(8,128)(2,1)S(1)} %get-tuple-element.48), channel_id=1, source_target_pairs={{16,0},{32,16},{48,32},{64,48},{80,64},{96,80},{112,96},{128,112},... | collective-permute-start | bytes 196616 | tf_op jit(solution)/shard_map/ppermute | solution.py:18
  204.9 1.9 collective-permute-start.12
  206.8 4.2 collective-permute-done.12
  211.1 1.9 collective-permute-start.15
  213.1 2.6 collective-permute-start.14
  216.3 10.5 %collective-permute-done.14 = bf16[6,1,128,128]{2,3,1,0:T(8,128)(2,1)S(1)} collective-permute-done((bf16[6,1,128,128]{2,3,1,0:T(8,128)(2,1)S(1)}, bf16[6,1,128,128]{2,3,1,0:T(8,128)(2,1)S(1)}, u32[]{:S(2)}, u32[]{:S(2)}) %collective-permute-start.14) | collective-permute-done | bytes 196640 | tf_op jit(solution)/shard_map/ppermute | solution.py:16
  230.8 1.3 gather_fusion.24
  232.1 1.3 gather_fusion.25
  233.4 1.3 gather_fusion.26
  236.0 1.8 copy.277
  237.8 1.3 convolution_multiply_fusion.6
  239.1 1.8 copy.278
  241.8 1.8 copy.280
  243.6 1.8 copy.281
  245.4 1.8 copy.282
  248.3 1.4 fusion.7
  249.7 1.4 fusion.6
  253.2 45.1 %all-reduce.1 = (f32[128]{0:T(128)S(1)}, f32[128]{0:T(128)S(1)}, f32[128]{0:T(128)S(1)}, f32[128]{0:T(128)S(1)}, f32[128]{0:T(128)S(1)}) all-reduce(f32[128]{0:T(128)S(1)} %get-tuple-element.13, f32[128]{0:T(128)S(1)} %get-tuple-element.10, f32[128]{0:T(128)S(1)} %get-tuple-element.11, ...), channel_id=1, replica_groups=mesh['gx'=32,'gy'=16] {'gy'}, use_global_device_ids=true, to_apply=%region_1.2 | all-reduce | flops 640 | bytes 5120 | tf_op jit(solution)/shard_map/psum | solution.py:64
  298.3 159.6 %all-reduce = (f32[1,128]{1,0:T(1,128)S(1)}, f32[1,128]{1,0:T(1,128)S(1)}, f32[1,128]{1,0:T(1,128)S(1)}, f32[1,128]{1,0:T(1,128)S(1)}, f32[1,128]{1,0:T(1,128)S(1)}) all-reduce(f32[1,128]{1,0:T(1,128)S(1)} %bitcast.255, f32[1,128]{1,0:T(1,128)S(1)} %bitcast.256, f32[1,128]{1,0:T(1,128)S(1)} %bitcast.257, ...), channel_id=1, replica_groups=mesh['gx'=32,'gy'=16] {'gx'}, use_global_device_ids=true, to_apply=%region_2.3 | all-reduce | flops 640 | bytes 5120 | tf_op jit(solution)/shard_map/psum | solution.py:64
  (246 shorter events, 48.6 us)
Async XLA Ops:
  1.5 16.4 %collective-permute-start = (bf16[1,2,128,128]{3,2,1,0:T(8,128)(2,1)S(1)}, bf16[1,2,128,128]{3,2,1,0:T(8,128)(2,1)S(1)}, u32[]{:S(2)}, u32[]{:S(2)}) collective-permute-start(bf16[1,2,128,128]{3,2,1,0:T(8,128)(2,1)S(1)} %get-tuple-element.54), channel_id=1, source_target_pairs={{0,16},{16,32},{32,48},{48,64},{64,80},{80,96},{96,112},{112,128},... | collective-permute-start | bytes 196616 | tf_op jit(solution)/shard_map/ppermute | solution.py:16
  5.0 13.9 %collective-permute-start.1 = (bf16[1,2,128,128]{3,2,1,0:T(8,128)(2,1)S(1)}, bf16[1,2,128,128]{3,2,1,0:T(8,128)(2,1)S(1)}, u32[]{:S(2)}, u32[]{:S(2)}) collective-permute-start(bf16[1,2,128,128]{3,2,1,0:T(8,128)(2,1)S(1)} %get-tuple-element.53), channel_id=1, source_target_pairs={{16,0},{32,16},{48,32},{64,48},{80,64},{96,80},{112,96},{128,112},... | collective-permute-start | bytes 196616 | tf_op jit(solution)/shard_map/ppermute | solution.py:18
  15.2 32.7 %copy-start.52 = (pred[4,2]{1,0:T(4,128)(4,1)}, pred[4,2]{1,0:T(4,128)(4,1)S(1)}, u32[]{:S(2)}) copy-start(pred[4,2]{1,0:T(4,128)(4,1)S(1)} %get-tuple-element.79) | copy-start | bytes 28
  15.2 36.7 %copy-start.50 = (pred[4,2]{1,0:T(4,128)(4,1)}, pred[4,2]{1,0:T(4,128)(4,1)S(1)}, u32[]{:S(2)}) copy-start(pred[4,2]{1,0:T(4,128)(4,1)S(1)} %get-tuple-element.26) | copy-start | bytes 28
  16.8 32.5 %copy-start.48 = (pred[4,2]{1,0:T(4,128)(4,1)}, pred[4,2]{1,0:T(4,128)(4,1)S(1)}, u32[]{:S(2)}) copy-start(pred[4,2]{1,0:T(4,128)(4,1)S(1)} %get-tuple-element.69) | copy-start | bytes 28
  16.9 33.9 %copy-start.46 = (pred[4,2]{1,0:T(4,128)(4,1)}, pred[4,2]{1,0:T(4,128)(4,1)S(1)}, u32[]{:S(2)}) copy-start(pred[4,2]{1,0:T(4,128)(4,1)S(1)} %get-tuple-element.71) | copy-start | bytes 28
  16.9 34.2 %copy-start.44 = (pred[4,2]{1,0:T(4,128)(4,1)}, pred[4,2]{1,0:T(4,128)(4,1)S(1)}, u32[]{:S(2)}) copy-start(pred[4,2]{1,0:T(4,128)(4,1)S(1)} %get-tuple-element.73) | copy-start | bytes 28
  16.9 34.6 %copy-start.42 = (pred[4,2]{1,0:T(4,128)(4,1)}, pred[4,2]{1,0:T(4,128)(4,1)S(1)}, u32[]{:S(2)}) copy-start(pred[4,2]{1,0:T(4,128)(4,1)S(1)} %get-tuple-element.75) | copy-start | bytes 28
  16.9 35.4 %copy-start.54 = (pred[4,2]{1,0:T(4,128)(4,1)}, pred[4,2]{1,0:T(4,128)(4,1)S(1)}, u32[]{:S(2)}) copy-start(pred[4,2]{1,0:T(4,128)(4,1)S(1)} %get-tuple-element.24) | copy-start | bytes 28
  17.8 34.5 %copy-start.26 = (f32[4,2]{1,0:T(4,128)}, f32[4,2]{1,0:T(4,128)S(1)}, u32[]{:S(2)}) copy-start(f32[4,2]{1,0:T(4,128)S(1)} %copy.253) | copy-start | bytes 100
  17.8 24.4 %copy-start.30 = (s32[1024]{0:T(1024)}, s32[1024]{0:T(1024)S(1)}, u32[]{:S(2)}) copy-start(s32[1024]{0:T(1024)S(1)} %get-tuple-element.105) | copy-start | bytes 12292
  17.8 25.7 %copy-start.28 = (s32[1024]{0:T(1024)}, s32[1024]{0:T(1024)S(1)}, u32[]{:S(2)}) copy-start(s32[1024]{0:T(1024)S(1)} %get-tuple-element.104) | copy-start | bytes 12292
  17.8 27.0 %copy-start.34 = (s32[1024]{0:T(1024)}, s32[1024]{0:T(1024)S(1)}, u32[]{:S(2)}) copy-start(s32[1024]{0:T(1024)S(1)} %get-tuple-element.103) | copy-start | bytes 12292
  17.8 28.3 %copy-start.32 = (s32[1024]{0:T(1024)}, s32[1024]{0:T(1024)S(1)}, u32[]{:S(2)}) copy-start(s32[1024]{0:T(1024)S(1)} %get-tuple-element.102) | copy-start | bytes 12292
  17.8 28.8 %copy-start.38 = (s32[1024]{0:T(1024)}, s32[1024]{0:T(1024)S(1)}, u32[]{:S(2)}) copy-start(s32[1024]{0:T(1024)S(1)} %get-tuple-element.101) | copy-start | bytes 12292
  17.9 29.4 %copy-start.36 = (s32[1024]{0:T(1024)}, s32[1024]{0:T(1024)S(1)}, u32[]{:S(2)}) copy-start(s32[1024]{0:T(1024)S(1)} %get-tuple-element.100) | copy-start | bytes 12292
  17.9 24.3 %copy-start.40 = (s32[1024]{0:T(1024)}, s32[1024]{0:T(1024)S(1)}, u32[]{:S(2)}) copy-start(s32[1024]{0:T(1024)S(1)} %pad_clamp_fusion.6) | copy-start | bytes 12292
  19.0 11.4 %collective-permute-start.3 = (bf16[6,1,128,128]{3,2,1,0:T(8,128)(2,1)S(1)}, bf16[6,1,128,128]{3,2,1,0:T(8,128)(2,1)S(1)}, u32[]{:S(2)}, u32[]{:S(2)}) collective-permute-start(bf16[6,1,128,128]{3,2,1,0:T(8,128)(2,1)S(1)} %get-tuple-element.46), channel_id=1, source_target_pairs={{1,0},{2,1},{3,2},{4,3},{5,4},{6,5},{7,6},{8,7},{9,8},{10,9},{11,1... | collective-permute-start | bytes 589832 | tf_op jit(solution)/shard_map/ppermute | solution.py:18
  27.2 13.6 %collective-permute-start.2 = (bf16[6,1,128,128]{3,2,1,0:T(8,128)(2,1)S(1)}, bf16[6,1,128,128]{3,2,1,0:T(8,128)(2,1)S(1)}, u32[]{:S(2)}, u32[]{:S(2)}) collective-permute-start(bf16[6,1,128,128]{3,2,1,0:T(8,128)(2,1)S(1)} %get-tuple-element.45), channel_id=1, source_target_pairs={{0,1},{1,2},{2,3},{3,4},{4,5},{5,6},{6,7},{7,8},{8,9},{9,10},{10,1... | collective-permute-start | bytes 589832 | tf_op jit(solution)/shard_map/ppermute | solution.py:16
  29.2 18.8 %copy-start.24 = (f32[4,2]{1,0:T(4,128)}, f32[4,2]{1,0:T(4,128)S(1)}, u32[]{:S(2)}) copy-start(f32[4,2]{1,0:T(4,128)S(1)} %get-tuple-element.64) | copy-start | bytes 100
  29.2 22.0 %copy-start.22 = (f32[4,2]{1,0:T(4,128)}, f32[4,2]{1,0:T(4,128)S(1)}, u32[]{:S(2)}) copy-start(f32[4,2]{1,0:T(4,128)S(1)} %get-tuple-element.63) | copy-start | bytes 100
  40.9 7.0 %copy-start = (bf16[4,2,7,128,128]{4,3,2,1,0:T(8,128)(2,1)S(1)}, bf16[4,2,7,128,128]{4,3,2,1,0:T(8,128)(2,1)}, u32[]{:S(2)}) copy-start(bf16[4,2,7,128,128]{4,3,2,1,0:T(8,128)(2,1)} %param.7) | copy-start | bytes 5505028
  47.9 2.8 copy-start.19
  49.3 1.8 copy-start.14
  52.3 33.5 %copy-start.4 = (bf16[4,2,128,128]{3,2,1,0:T(8,128)(2,1)S(1)}, bf16[4,2,128,128]{3,2,1,0:T(8,128)(2,1)}, u32[]{:S(2)}) copy-start(bf16[4,2,128,128]{3,2,1,0:T(8,128)(2,1)} %param.6) | copy-start | bytes 786436
  52.7 17.2 %collective-permute-start.5 = (bf16[1,2,128,128]{2,3,1,0:T(8,128)(2,1)S(1)}, bf16[1,2,128,128]{2,3,1,0:T(8,128)(2,1)S(1)}, u32[]{:S(2)}, u32[]{:S(2)}) collective-permute-start(bf16[1,2,128,128]{2,3,1,0:T(8,128)(2,1)S(1)} %get-tuple-element.52), channel_id=1, source_target_pairs={{16,0},{32,16},{48,32},{64,48},{80,64},{96,80},{112,96},{128,112},... | collective-permute-start | bytes 196616 | tf_op jit(solution)/shard_map/ppermute | solution.py:18
  68.0 12.7 %collective-permute-start.4 = (bf16[1,2,128,128]{2,3,1,0:T(8,128)(2,1)S(1)}, bf16[1,2,128,128]{2,3,1,0:T(8,128)(2,1)S(1)}, u32[]{:S(2)}, u32[]{:S(2)}) collective-permute-start(bf16[1,2,128,128]{2,3,1,0:T(8,128)(2,1)S(1)} %get-tuple-element.51), channel_id=1, source_target_pairs={{0,16},{16,32},{32,48},{48,64},{64,80},{80,96},{96,112},{112,128},... | collective-permute-start | bytes 196616 | tf_op jit(solution)/shard_map/ppermute | solution.py:16
  81.5 5.9 %collective-permute-start.7 = (bf16[6,1,128,128]{2,3,1,0:T(8,128)(2,1)}, bf16[6,1,128,128]{2,3,1,0:T(8,128)(2,1)S(1)}, u32[]{:S(2)}, u32[]{:S(2)}) collective-permute-start(bf16[6,1,128,128]{2,3,1,0:T(8,128)(2,1)} %get-tuple-element.44), channel_id=1, source_target_pairs={{1,0},{2,1},{3,2},{4,3},{5,4},{6,5},{7,6},{8,7},{9,8},{10,9},{11,1... | collective-permute-start | bytes 589832 | tf_op jit(solution)/shard_map/ppermute | solution.py:18
  83.4 13.7 %collective-permute-start.6 = (bf16[6,1,128,128]{2,3,1,0:T(8,128)(2,1)S(1)}, bf16[6,1,128,128]{2,3,1,0:T(8,128)(2,1)}, u32[]{:S(2)}, u32[]{:S(2)}) collective-permute-start(bf16[6,1,128,128]{2,3,1,0:T(8,128)(2,1)S(1)} %get-tuple-element.43), channel_id=1, source_target_pairs={{0,1},{1,2},{2,3},{3,4},{4,5},{5,6},{6,7},{7,8},{8,9},{9,10},{10,1... | collective-permute-start | bytes 589832 | tf_op jit(solution)/shard_map/ppermute | solution.py:16
  98.2 7.9 %copy-start.37 = (s32[1024]{0:T(1024)S(1)}, s32[1024]{0:T(1024)}, u32[]{:S(2)}) copy-start(s32[1024]{0:T(1024)} %copy-done.36) | copy-start | bytes 12292
  99.0 9.3 %copy-start.25 = (f32[4,2]{1,0:T(4,128)S(1)}, f32[4,2]{1,0:T(4,128)}, u32[]{:S(2)}) copy-start(f32[4,2]{1,0:T(4,128)} %copy-done.24) | copy-start | bytes 100
  99.0 9.3 %copy-start.53 = (pred[4,2]{1,0:T(4,128)(4,1)S(1)}, pred[4,2]{1,0:T(4,128)(4,1)}, u32[]{:S(2)}) copy-start(pred[4,2]{1,0:T(4,128)(4,1)} %copy-done.52) | copy-start | bytes 28
  107.4 9.5 %copy-start.7 = (bf16[8,128,128]{1,2,0:T(8,128)(2,1)S(1)}, bf16[8,128,128]{1,2,0:T(8,128)(2,1)}, u32[]{:S(2)}) copy-start(bf16[8,128,128]{1,2,0:T(8,128)(2,1)} %gather_fusion.12) | copy-start | bytes 786436
  108.3 9.5 %copy-start.6 = (bf16[8,128,128]{1,2,0:T(8,128)(2,1)S(1)}, bf16[8,128,128]{1,2,0:T(8,128)(2,1)}, u32[]{:S(2)}) copy-start(bf16[8,128,128]{1,2,0:T(8,128)(2,1)} %gather_fusion.13) | copy-start | bytes 786436
  109.6 9.0 %copy-start.49 = (pred[4,2]{1,0:T(4,128)(4,1)S(1)}, pred[4,2]{1,0:T(4,128)(4,1)}, u32[]{:S(2)}) copy-start(pred[4,2]{1,0:T(4,128)(4,1)} %copy-done.48) | copy-start | bytes 28
  113.3 6.7 %copy-start.47 = (pred[4,2]{1,0:T(4,128)(4,1)S(1)}, pred[4,2]{1,0:T(4,128)(4,1)}, u32[]{:S(2)}) copy-start(pred[4,2]{1,0:T(4,128)(4,1)} %copy-done.46) | copy-start | bytes 28
  117.8 3.6 copy-start.17
  117.8 3.6 copy-start.23
  117.8 3.6 copy-start.45
  120.0 1.9 copy-start.15
  120.0 1.9 copy-start.43
  121.8 1.0 copy-start.20
  124.1 39.0 %copy-start.41 = (s32[1024]{0:T(1024)S(1)}, s32[1024]{0:T(1024)}, u32[]{:S(2)}) copy-start(s32[1024]{0:T(1024)} %copy-done.40) | copy-start | bytes 12292
  124.1 19.0 %collective-permute-start.9 = (bf16[1,2,128,128]{2,3,1,0:T(8,128)(2,1)S(1)}, bf16[1,2,128,128]{2,3,1,0:T(8,128)(2,1)S(1)}, u32[]{:S(2)}, u32[]{:S(2)}) collective-permute-start(bf16[1,2,128,128]{2,3,1,0:T(8,128)(2,1)S(1)} %get-tuple-element.50), channel_id=1, source_target_pairs={{16,0},{32,16},{48,32},{64,48},{80,64},{96,80},{112,96},{128,112},... | collective-permute-start | bytes 196616 | tf_op jit(solution)/shard_map/ppermute | solution.py:18
  141.2 23.2 %copy-start.31 = (s32[1024]{0:T(1024)S(1)}, s32[1024]{0:T(1024)}, u32[]{:S(2)}) copy-start(s32[1024]{0:T(1024)} %copy-done.30) | copy-start | bytes 12292
  141.2 6.2 %collective-permute-start.8 = (bf16[1,2,128,128]{2,3,1,0:T(8,128)(2,1)S(1)}, bf16[1,2,128,128]{2,3,1,0:T(8,128)(2,1)S(1)}, u32[]{:S(2)}, u32[]{:S(2)}) collective-permute-start(bf16[1,2,128,128]{2,3,1,0:T(8,128)(2,1)S(1)} %get-tuple-element.49), channel_id=1, source_target_pairs={{0,16},{16,32},{32,48},{48,64},{64,80},{80,96},{96,112},{112,128},... | collective-permute-start | bytes 196616 | tf_op jit(solution)/shard_map/ppermute | solution.py:16
  147.4 18.3 %copy-start.29 = (s32[1024]{0:T(1024)S(1)}, s32[1024]{0:T(1024)}, u32[]{:S(2)}) copy-start(s32[1024]{0:T(1024)} %copy-done.28) | copy-start | bytes 12292
  147.4 19.6 %copy-start.35 = (s32[1024]{0:T(1024)S(1)}, s32[1024]{0:T(1024)}, u32[]{:S(2)}) copy-start(s32[1024]{0:T(1024)} %copy-done.34) | copy-start | bytes 12292
  147.5 5.4 %collective-permute-start.11 = (bf16[6,1,128,128]{2,3,1,0:T(8,128)(2,1)S(1)}, bf16[6,1,128,128]{2,3,1,0:T(8,128)(2,1)S(1)}, u32[]{:S(2)}, u32[]{:S(2)}) collective-permute-start(bf16[6,1,128,128]{2,3,1,0:T(8,128)(2,1)S(1)} %get-tuple-element.42), channel_id=1, source_target_pairs={{1,0},{2,1},{3,2},{4,3},{5,4},{6,5},{7,6},{8,7},{9,8},{10,9},{11,1... | collective-permute-start | bytes 589832 | tf_op jit(solution)/shard_map/ppermute | solution.py:18
  149.4 18.9 %copy-start.33 = (s32[1024]{0:T(1024)S(1)}, s32[1024]{0:T(1024)}, u32[]{:S(2)}) copy-start(s32[1024]{0:T(1024)} %copy-done.32) | copy-start | bytes 12292
  149.4 20.2 %copy-start.39 = (s32[1024]{0:T(1024)S(1)}, s32[1024]{0:T(1024)}, u32[]{:S(2)}) copy-start(s32[1024]{0:T(1024)} %copy-done.38) | copy-start | bytes 12292
  149.4 13.6 %collective-permute-start.10 = (bf16[6,1,128,128]{2,3,1,0:T(8,128)(2,1)S(1)}, bf16[6,1,128,128]{2,3,1,0:T(8,128)(2,1)S(1)}, u32[]{:S(2)}, u32[]{:S(2)}) collective-permute-start(bf16[6,1,128,128]{2,3,1,0:T(8,128)(2,1)S(1)} %get-tuple-element.41), channel_id=1, source_target_pairs={{0,1},{1,2},{2,3},{3,4},{4,5},{5,6},{6,7},{7,8},{8,9},{9,10},{10,1... | collective-permute-start | bytes 589832 | tf_op jit(solution)/shard_map/ppermute | solution.py:16
  172.2 10.4 %copy-start.8 = (bf16[8,128,128]{1,2,0:T(8,128)(2,1)S(1)}, bf16[8,128,128]{1,2,0:T(8,128)(2,1)}, u32[]{:S(2)}) copy-start(bf16[8,128,128]{1,2,0:T(8,128)(2,1)} %gather_fusion.19) | copy-start | bytes 786436
  184.6 2.8 copy-start.18
  186.0 1.8 copy-start.16
  189.9 16.9 %collective-permute-start.13 = (bf16[1,2,128,128]{2,3,1,0:T(8,128)(2,1)S(1)}, bf16[1,2,128,128]{2,3,1,0:T(8,128)(2,1)S(1)}, u32[]{:S(2)}, u32[]{:S(2)}) collective-permute-start(bf16[1,2,128,128]{2,3,1,0:T(8,128)(2,1)S(1)} %get-tuple-element.48), channel_id=1, source_target_pairs={{16,0},{32,16},{48,32},{64,48},{80,64},{96,80},{112,96},{128,112},... | collective-permute-start | bytes 196616 | tf_op jit(solution)/shard_map/ppermute | solution.py:18
  204.9 6.2 %collective-permute-start.12 = (bf16[1,2,128,128]{2,3,1,0:T(8,128)(2,1)S(1)}, bf16[1,2,128,128]{2,3,1,0:T(8,128)(2,1)S(1)}, u32[]{:S(2)}, u32[]{:S(2)}) collective-permute-start(bf16[1,2,128,128]{2,3,1,0:T(8,128)(2,1)S(1)} %get-tuple-element.47), channel_id=1, source_target_pairs={{0,16},{16,32},{32,48},{48,64},{64,80},{80,96},{96,112},{112,128},... | collective-permute-start | bytes 196616 | tf_op jit(solution)/shard_map/ppermute | solution.py:16
  211.1 5.2 %collective-permute-start.15 = (bf16[6,1,128,128]{2,3,1,0:T(8,128)(2,1)S(1)}, bf16[6,1,128,128]{2,3,1,0:T(8,128)(2,1)S(1)}, u32[]{:S(2)}, u32[]{:S(2)}) collective-permute-start(bf16[6,1,128,128]{2,3,1,0:T(8,128)(2,1)S(1)} %get-tuple-element.40), channel_id=1, source_target_pairs={{1,0},{2,1},{3,2},{4,3},{5,4},{6,5},{7,6},{8,7},{9,8},{10,9},{11,1... | collective-permute-start | bytes 589832 | tf_op jit(solution)/shard_map/ppermute | solution.py:18
  213.1 13.8 %collective-permute-start.14 = (bf16[6,1,128,128]{2,3,1,0:T(8,128)(2,1)S(1)}, bf16[6,1,128,128]{2,3,1,0:T(8,128)(2,1)S(1)}, u32[]{:S(2)}, u32[]{:S(2)}) collective-permute-start(bf16[6,1,128,128]{2,3,1,0:T(8,128)(2,1)S(1)} %get-tuple-element.39), channel_id=1, source_target_pairs={{0,1},{1,2},{2,3},{3,4},{4,5},{5,6},{6,7},{7,8},{8,9},{9,10},{10,1... | collective-permute-start | bytes 589832 | tf_op jit(solution)/shard_map/ppermute | solution.py:16
  236.0 5.0 %copy-start.5 = (bf16[8,128,128]{1,2,0:T(8,128)(2,1)S(1)}, bf16[8,128,128]{1,2,0:T(8,128)(2,1)}, u32[]{:S(2)}) copy-start(bf16[8,128,128]{1,2,0:T(8,128)(2,1)} %gather_fusion.23) | copy-start | bytes 786436
  248.3 2.8 copy-start.11
  249.7 1.8 copy-start.10
  251.5 1.1 copy-start.2
  251.5 1.2 copy-start.3
  (8 other events, 7.5 us)
